TPU v7x, 128 devices: a whole 4x4x4 slice. The times are simulated.
128 devices in a mesh: section: 2 (over x_hi), wide: 64 (over x_lo, y, z, core).
Axes of the slice: x: 4 (x_hi: 2, x_lo: 2; x = x_hi * 2 + x_lo), y: 4, z: 4, core: 2. Of those that a mesh axis runs over, the one named last changes fastest.
Arguments:
- section_ends: bfloat16 [2, 2, 4096, 768], P('section', None, 'wide'), may hold values from -6 to 6
- qkv_weight: bfloat16 [2, 768, 2304], P('section', 'wide'), may hold values from -0.21875 to 0.21875
- attn_weight: bfloat16 [2, 768, 768], P('section', 'wide'), may hold values from -0.625 to 0.625
- route_weight: bfloat16 [2, 768, 32], P('section', 'wide'), may hold values from -0.15625 to 0.15625
- norm_gains: bfloat16 [2, 2, 768], P('section', None, 'wide'), may hold values from 0.5 to 1.5
- norm_shifts: bfloat16 [2, 2, 768], P('section', None, 'wide'), may hold values from -2 to 2
- expert_in: bfloat16 [2, 64, 768, 1536], P('section', 'wide'), may hold values from -0.21875 to 0.21875
- expert_out: bfloat16 [2, 64, 1536, 768], P('section', 'wide'), may hold values from -0.109375 to 0.109375
- routes: int32 [2, 2, 4096, 2], P('section', None, 'wide'), may hold values from 0 to 31, all different within a row; in each aligned block of 64 rows (0 to 63, 64 to 127, ..., all dimensions but the last counted through in order) at most 8 rows name the same one
Outputs:
- ends_out: bfloat16 [2, 2, 4096, 768], P('section', None, 'wide')
- qkv_grad: float32 [2, 768, 2304], P('section', 'wide')
- attn_grad: float32 [2, 768, 768], P('section', 'wide')
- route_grad: float32 [2, 768, 32], P('section', 'wide')
- gain_grad: float32 [2, 2, 768], P('section', None, 'wide')
- shift_grad: float32 [2, 2, 768], P('section', None, 'wide')
- expert_in_grad: float32 [2, 64, 768, 1536], P('section', 'wide')
- expert_out_grad: float32 [2, 64, 1536, 768], P('section', 'wide')
Inputs may be any that keep to these rules, and one draw needn't show every extreme that they name: `routes`: within each layer and micro-batch, the 64 rows of one device name each expert at most 8 times, a bound that some block reaches; the two experts of a row differ.
All inputs are finite; a program needn't handle non-finite values.
Results may differ from a plain program's by a relative error of at most 0.015.
Values may be sent and summed in bfloat16 or wider, within the bound.
A program may use at most 192 MiB of HBM per device.

v0:
```python
from functools import partial

import jax
import jax.numpy as jnp
from jax import lax
from jax.sharding import PartitionSpec as P

HEADS = 12
HD = 64


EPSILON = 1e-06
PRECISE = lax.Precision.HIGHEST


def shifted(value, axis, steps):
    count = lax.axis_size(axis)
    initial, last = (max(0, -steps), min(count, count - steps))
    return lax.ppermute(value, axis, [(source, source + steps) for source in range(initial, last)])


def normalize(values, gain_row, shift_row):
    centered = values - jnp.mean(values, axis=-1, keepdims=True)
    inverse = lax.rsqrt(jnp.mean(centered * centered, axis=-1, keepdims=True) + EPSILON)
    unit_rows = centered * inverse
    return (unit_rows * gain_row + shift_row, unit_rows, inverse)


def normalize_back(grad_rows, unit_rows, inverse, gain_row):
    scaled = grad_rows * gain_row
    inner = (
        scaled
        - jnp.mean(scaled, axis=-1, keepdims=True)
        - unit_rows * jnp.mean(scaled * unit_rows, axis=-1, keepdims=True)
    )
    return (inner * inverse, jnp.sum(grad_rows * unit_rows, axis=0), jnp.sum(grad_rows, axis=0))


def build_slots(route_rows, experts, capacity):
    assigned = route_rows.reshape(-1)
    onehot = (assigned[:, None] == jnp.arange(experts, dtype=jnp.int32)[None, :]).astype(jnp.int32)
    earlier = jnp.cumsum(onehot, axis=0) - onehot
    position = jnp.sum(earlier * onehot, axis=1)
    in_slot = (position[None, :] == jnp.arange(capacity, dtype=jnp.int32)[:, None]).astype(
        jnp.int32
    )
    return (onehot.T[:, None, :] * in_slot[None, :, :]).astype(jnp.bfloat16)


def fetch_dense(qkv_weight, attn_weight, route_weight, norm_gains, norm_shifts):
    gathered = (
        lax.all_gather(qkv_weight, "wide", axis=1, tiled=True),
        lax.all_gather(attn_weight, "wide", axis=1, tiled=True),
        lax.all_gather(route_weight, "wide", axis=1, tiled=True),
        lax.all_gather(norm_gains, "wide", axis=2, tiled=True),
        lax.all_gather(norm_shifts, "wide", axis=2, tiled=True),
    )
    return tuple((piece[0] for piece in gathered))


def add_tuples(left_terms, right_terms):
    return tuple(
        (first_term + second_term for first_term, second_term in zip(left_terms, right_terms))
    )


def forward_layer(stream, dense_now, weight_in, weight_out, route_rows):
    weight_qkv, weight_attn, weight_route, gain_rows, shift_rows = dense_now
    tokens, model_width = stream.shape
    experts = weight_route.shape[1]
    capacity = 4 * tokens // experts
    scaling = HD ** (-0.5)
    normed_one, unit_one, inverse_one = normalize(
        stream, gain_rows[0].astype(jnp.float32), shift_rows[0].astype(jnp.float32)
    )
    entering = normed_one.astype(jnp.bfloat16)
    projected = jnp.dot(entering, weight_qkv, preferred_element_type=jnp.float32).astype(
        jnp.bfloat16
    )
    projected = projected.reshape(tokens, 3, HEADS, HD)
    queries, keys_in, values_in = (projected[:, 0], projected[:, 1], projected[:, 2])
    scores = (
        jnp.einsum("qhd,khd->hqk", queries, keys_in, preferred_element_type=jnp.float32) * scaling
    )
    row_peak = jnp.max(scores, axis=-1, keepdims=True)
    log_total = row_peak + jnp.log(jnp.sum(jnp.exp(scores - row_peak), axis=-1, keepdims=True))
    weights = jnp.exp(scores - log_total).astype(jnp.bfloat16)
    attended = jnp.einsum("hqk,khd->qhd", weights, values_in, preferred_element_type=jnp.float32)
    attended = attended.astype(jnp.bfloat16).reshape(tokens, model_width)
    hidden = stream + jnp.dot(attended, weight_attn, preferred_element_type=jnp.float32)
    normed_two, unit_two, inverse_two = normalize(
        hidden, gain_rows[1].astype(jnp.float32), shift_rows[1].astype(jnp.float32)
    )
    leaving = normed_two.astype(jnp.bfloat16)
    logits = jnp.dot(leaving, weight_route, preferred_element_type=jnp.float32)
    chosen = (route_rows[:, :, None] == jnp.arange(experts, dtype=jnp.int32)).astype(jnp.float32)
    gate_rows = jax.nn.softmax(jnp.sum(chosen * logits[:, None, :], axis=2), axis=-1)
    slot_map = build_slots(route_rows, experts, capacity)
    doubled = jnp.repeat(leaving, 2, axis=0)
    outgoing = jnp.einsum(
        "eca,ad->ecd", slot_map, doubled, preferred_element_type=jnp.float32
    ).astype(jnp.bfloat16)
    outgoing = jnp.repeat(outgoing, 2, axis=0)
    arrived = lax.all_to_all(outgoing, "wide", split_axis=0, concat_axis=0, tiled=True)
    raised = jnp.einsum("ncd,df->ncf", arrived, weight_in, preferred_element_type=jnp.float32)
    activated = jax.nn.gelu(raised, approximate=False).astype(jnp.bfloat16)
    partial_out = jnp.einsum(
        "ncf,fd->ncd", activated, weight_out, preferred_element_type=jnp.float32
    ).astype(jnp.bfloat16)
    returned = lax.all_to_all(partial_out, "wide", split_axis=0, concat_axis=0, tiled=True)
    returned, arrived, raised = (returned, arrived, raised)
    halves = returned.reshape(experts, 2, capacity, model_width)
    combined = jnp.einsum("eca,ehcd->had", slot_map, halves, preferred_element_type=jnp.float32)
    combined = (combined[0] + combined[1]).reshape(tokens, 2, model_width)
    output = hidden + jnp.sum(gate_rows[:, :, None] * combined, axis=1)
    stored = (
        unit_one,
        inverse_one,
        entering,
        projected,
        log_total,
        attended,
        unit_two,
        inverse_two,
        leaving,
        gate_rows,
        combined,
        slot_map,
        chosen,
        arrived,
        raised,
    )
    return (output, stored)


def backward_layer(grad_out, stored, dense_now, weight_in, weight_out):
    weight_qkv, weight_attn, weight_route, gain_rows, shift_rows = dense_now
    (
        unit_one,
        inverse_one,
        entering,
        projected,
        log_total,
        attended,
        unit_two,
        inverse_two,
        leaving,
        gate_rows,
        combined,
        slot_map,
        chosen,
        arrived,
        raised,
    ) = stored
    tokens, model_width = grad_out.shape
    experts = weight_route.shape[1]
    capacity = slot_map.shape[1]
    scaling = HD ** (-0.5)
    gate_grad = jnp.sum(combined * grad_out[:, None, :], axis=2)
    logit_pair = gate_rows * (gate_grad - jnp.sum(gate_rows * gate_grad, axis=1, keepdims=True))
    logit_grad = jnp.sum(chosen * logit_pair[:, :, None], axis=1)
    route_grad = jnp.einsum("td,te->de", leaving.astype(jnp.float32), logit_grad, precision=PRECISE)
    leaving_grad = jnp.einsum(
        "te,de->td", logit_grad, weight_route.astype(jnp.float32), precision=PRECISE
    )
    part_grad = (
        (gate_rows[:, :, None] * grad_out[:, None, :])
        .reshape(2 * tokens, model_width)
        .astype(jnp.bfloat16)
    )
    outgoing = jnp.einsum(
        "eca,ad->ecd", slot_map, part_grad, preferred_element_type=jnp.float32
    ).astype(jnp.bfloat16)
    outgoing = jnp.repeat(outgoing, 2, axis=0)
    incoming = lax.all_to_all(outgoing, "wide", split_axis=0, concat_axis=0, tiled=True)
    activated = jax.nn.gelu(raised, approximate=False).astype(jnp.bfloat16)
    out_grad = jnp.einsum("ncf,ncd->fd", activated, incoming, preferred_element_type=jnp.float32)
    act_grad = jnp.einsum("ncd,fd->ncf", incoming, weight_out, preferred_element_type=jnp.float32)
    gelu_back = jax.vjp(partial(jax.nn.gelu, approximate=False), raised)[1]
    raised_grad = gelu_back(act_grad)[0].astype(jnp.bfloat16)
    in_grad = jnp.einsum("ncd,ncf->df", arrived, raised_grad, preferred_element_type=jnp.float32)
    row_grad = jnp.einsum(
        "ncf,df->ncd", raised_grad, weight_in, preferred_element_type=jnp.float32
    ).astype(jnp.bfloat16)
    coming_back = lax.all_to_all(row_grad, "wide", split_axis=0, concat_axis=0, tiled=True)
    halves = coming_back.reshape(experts, 2, capacity, model_width)
    token_grad = jnp.einsum("eca,ehcd->had", slot_map, halves, preferred_element_type=jnp.float32)
    token_grad = (token_grad[0] + token_grad[1]).reshape(tokens, 2, model_width)
    leaving_grad = leaving_grad + jnp.sum(token_grad, axis=1)
    normed_grad, gain_two, shift_two = normalize_back(
        leaving_grad, unit_two, inverse_two, gain_rows[1].astype(jnp.float32)
    )
    hidden_grad = grad_out + normed_grad
    branch_grad = hidden_grad.astype(jnp.bfloat16)
    attn_grad = jnp.einsum("td,te->de", attended, branch_grad, preferred_element_type=jnp.float32)
    attended_grad = jnp.einsum(
        "te,de->td", branch_grad, weight_attn, preferred_element_type=jnp.float32
    )
    attended_grad = attended_grad.astype(jnp.bfloat16).reshape(tokens, HEADS, HD)
    queries, keys_in, values_in = (projected[:, 0], projected[:, 1], projected[:, 2])
    scores = (
        jnp.einsum("qhd,khd->hqk", queries, keys_in, preferred_element_type=jnp.float32) * scaling
    )
    probs = jnp.exp(scores - log_total)
    weights = probs.astype(jnp.bfloat16)
    value_grad = jnp.einsum(
        "hqk,qhd->khd", weights, attended_grad, preferred_element_type=jnp.float32
    )
    prob_grad = jnp.einsum(
        "qhd,khd->hqk", attended_grad, values_in, preferred_element_type=jnp.float32
    )
    score_grad = (probs * (prob_grad - jnp.sum(probs * prob_grad, axis=-1, keepdims=True))).astype(
        jnp.bfloat16
    )
    query_grad = (
        jnp.einsum("hqk,khd->qhd", score_grad, keys_in, preferred_element_type=jnp.float32)
        * scaling
    )
    key_grad = (
        jnp.einsum("hqk,qhd->khd", score_grad, queries, preferred_element_type=jnp.float32)
        * scaling
    )
    projected_grad = (
        jnp.stack([query_grad, key_grad, value_grad], axis=1)
        .reshape(tokens, 3 * model_width)
        .astype(jnp.bfloat16)
    )
    qkv_grad = jnp.einsum("td,te->de", entering, projected_grad, preferred_element_type=jnp.float32)
    entering_grad = jnp.einsum(
        "te,de->td", projected_grad, weight_qkv, preferred_element_type=jnp.float32
    )
    normed_grad, gain_one, shift_one = normalize_back(
        entering_grad, unit_one, inverse_one, gain_rows[0].astype(jnp.float32)
    )
    stream_grad = hidden_grad + normed_grad
    dense_grads = (
        qkv_grad,
        attn_grad,
        route_grad,
        jnp.stack([gain_one, gain_two]),
        jnp.stack([shift_one, shift_two]),
    )
    return (stream_grad, dense_grads, (in_grad, out_grad))


def body(
    section_ends,
    qkv_weight,
    attn_weight,
    route_weight,
    norm_gains,
    norm_shifts,
    expert_in,
    expert_out,
    routes,
):
    shards = (qkv_weight, attn_weight, route_weight, norm_gains, norm_shifts)
    ends_here = section_ends[0]
    route_here = routes[0]
    batches = ends_here.shape[0]
    section_number = lax.axis_index("section")
    leading = section_number == 0
    weight_in = expert_in[0, 0]
    weight_out = expert_out[0, 0]
    arriving = jnp.zeros(ends_here.shape[1:], jnp.bfloat16)
    stored_all = []
    produced = []
    for tick_num in range(batches + 1):
        dense_now = fetch_dense(*shards)
        batch_pick = jnp.clip(tick_num - section_number, 0, batches - 1)
        route_now = lax.dynamic_index_in_dim(route_here, batch_pick, 0, keepdims=False)
        entering = jnp.where(leading, ends_here[min(tick_num, batches - 1)], arriving).astype(
            jnp.float32
        )
        output, stored = forward_layer(entering, dense_now, weight_in, weight_out, route_now)
        stored_all.append(stored)
        leaving = output.astype(jnp.bfloat16)
        if tick_num > 0:
            produced.append(leaving)
        if tick_num < batches:
            arriving = shifted(leaving, "section", 1)
    arriving = jnp.zeros(ends_here.shape[1:], jnp.bfloat16)
    input_grads = []
    dense_sum = None
    expert_in_sum = jnp.zeros(weight_in.shape, jnp.float32)
    expert_out_sum = jnp.zeros(weight_out.shape, jnp.float32)
    for tick_num in range(batches + 1):
        dense_now = fetch_dense(*shards)
        batch_raw = tick_num - 1 + section_number
        usable = ((batch_raw >= 0) & (batch_raw < batches)).astype(jnp.float32)
        stored = jax.tree.map(
            lambda early_one, later_one: jnp.where(leading, early_one, later_one),
            stored_all[max(tick_num - 1, 0)],
            stored_all[min(tick_num + 1, batches)],
        )
        grad_out = jnp.where(leading, arriving, ends_here[min(tick_num, batches - 1)]).astype(
            jnp.float32
        )
        stream_grad, dense_grads, expert_grads = backward_layer(
            grad_out, stored, dense_now, weight_in, weight_out
        )
        sent_back = stream_grad.astype(jnp.bfloat16)
        if tick_num > 0:
            input_grads.append(sent_back)
        if tick_num < batches:
            arriving = shifted(sent_back, "section", -1)
        expert_in_sum = expert_in_sum + usable * expert_grads[0]
        expert_out_sum = expert_out_sum + usable * expert_grads[1]
        grad_qkv = (usable * dense_grads[0])[None]
        grad_attn = (usable * dense_grads[1])[None]
        grad_route = (usable * dense_grads[2])[None]
        grad_gain = (usable * dense_grads[3])[None]
        grad_shift = (usable * dense_grads[4])[None]
        shares = (
            lax.psum_scatter(grad_qkv, "wide", scatter_dimension=1, tiled=True),
            lax.psum_scatter(grad_attn, "wide", scatter_dimension=1, tiled=True),
            lax.psum_scatter(grad_route, "wide", scatter_dimension=1, tiled=True),
            lax.psum_scatter(grad_gain, "wide", scatter_dimension=2, tiled=True),
            lax.psum_scatter(grad_shift, "wide", scatter_dimension=2, tiled=True),
        )
        dense_sum = shares if dense_sum is None else add_tuples(dense_sum, shares)
    finished = jnp.where(leading, jnp.stack(input_grads), jnp.stack(produced))[None]
    return (
        finished,
        dense_sum[0],
        dense_sum[1],
        dense_sum[2],
        dense_sum[3],
        dense_sum[4],
        expert_in_sum[None, None],
        expert_out_sum[None, None],
    )


def solution(mesh):
    return jax.shard_map(
        body,
        mesh=mesh,
        in_specs=(
            P("section", None, "wide", None),
            P("section", "wide", None),
            P("section", "wide", None),
            P("section", "wide", None),
            P("section", None, "wide"),
            P("section", None, "wide"),
            P("section", "wide", None, None),
            P("section", "wide", None, None),
            P("section", None, "wide", None),
        ),
        out_specs=(
            P("section", None, "wide", None),
            P("section", "wide", None),
            P("section", "wide", None),
            P("section", "wide", None),
            P("section", None, "wide"),
            P("section", None, "wide"),
            P("section", "wide", None, None),
            P("section", "wide", None, None),
        ),
        check_vma=False,
    )
```

profile of v0, /device:TPU:0, one launch (start us, length us, event | category | flops | bytes accessed | tf_op | source)
XLA Modules:
  0.0 1490.1 jit_solution(6340218135140407994)
XLA Ops:
  14.2 84.9 %all_gather.11 = bf16[1,2,768]{1,0,2:T(2,128)(2,1)S(1)} all-gather(bf16[1,2,12]{1,0,2:T(2,128)(2,1)S(1)} %copy.338), channel_id=1, replica_groups=mesh['section'=2,'wide'=64] {'wide'}, dimensions={2}, use_global_device_ids=true | all-gather | bytes 3120 | tf_op jit(solution)/shard_map/all_gather | solution.py:56
  99.1 77.6 %all_gather.10 = bf16[1,2,768]{1,0,2:T(2,128)(2,1)S(1)} all-gather(bf16[1,2,12]{1,0,2:T(2,128)(2,1)S(1)} %copy.337), channel_id=1, replica_groups=mesh['section'=2,'wide'=64] {'wide'}, dimensions={2}, use_global_device_ids=true | all-gather | bytes 3120 | tf_op jit(solution)/shard_map/all_gather | solution.py:55
  179.5 4.6 fusion.268
  184.1 4.6 fusion.269
  191.8 36.3 %all-gather.3.cloned.1.call-done = bf16[1,768,2304]{2,0,1:T(2,128)(2,1)} async-done(((bf16[1,12,2304]{2,0,1:T(2,128)(2,1)}), bf16[1,768,2304]{2,0,1:T(2,128)(2,1)}) %all-gather.3.cloned.1.call-update) | async-done | bytes 3538960 | tf_op jit(solution)/shard_map/all_gather | solution.py:52
  228.2 3.6 copy.455
  253.0 6.4 all-to-all-start
  266.6 88.6 %all_gather.14 = bf16[1,768,32]{2,0,1:T(2,128)(2,1)} all-gather(bf16[1,12,32]{2,0,1:T(2,128)(2,1)} %copy.345), channel_id=1, replica_groups=mesh['section'=2,'wide'=64] {'wide'}, dimensions={1}, use_global_device_ids=true | all-gather | bytes 49920 | tf_op jit(solution)/shard_map/all_gather | solution.py:54
  358.2 2.7 fusion.94
  362.5 9.1 fusion.191
  371.6 5.5 all-to-all-start.1
  386.1 5.0 all-to-all-done.1
  398.7 4.8 collective-permute-start
  408.5 3.5 fusion.21
  416.1 2.7 broadcast_select_fusion.5
  432.4 5.7 all-to-all-start.2
  447.1 5.1 all-to-all-done.2
  452.2 2.7 fusion.92
  456.6 9.1 fusion.196
  465.7 5.9 all-to-all-start.3
  491.6 2.7 multiply_reduce_fusion.7
  509.6 5.2 collective-permute-start.2
  521.6 3.5 fusion.24
  529.1 2.5 broadcast_select_fusion.3
  545.5 8.5 all-to-all-start.6
  563.9 4.1 all-to-all-done.6
  570.0 6.3 all-to-all-start.4
  576.3 17.3 %fusion.37 = (f32[64,8,1536]{2,1,0:T(8,128)}, f32[64,8,1536]{2,1,0:T(8,128)}, f32[64,8,1536]{2,1,0:T(8,128)}, f32[64,8,1536]{2,1,0:T(8,128)}, f32[64,8,1536]{2,1,0:T(8,128)}) fusion(f32[64,8,1536]{2,1,0:T(8,128)} %copy-done.130, pred[]{:T(512)S(6)} %eq.177, f32[64,8,1536]{2,1,0:T(8,128)} %copy-done.128, bf16[64,8,768]{2,1,0:T(8,128)(2,1)} %all-to-all-done.6, ...), kind=kOutput, calls=%fused_computation.44 | convolution fusion | flops 1307049984 | bytes 25165824 | tf_op jit(solution)/shard_map/ncd,df->ncf/dot_general | solution.py:105
  593.7 5.9 add_convert_fusion.2
  600.7 2.3 fusion.206
  603.0 9.1 all-to-all-start.5
  612.1 6.7 fusion.96
  618.9 9.0 fusion.201
  627.9 9.1 all-to-all-start.7
  655.8 2.3 convert_element_type.443
  658.2 4.0 multiply_reduce_fusion.14
  664.3 2.3 convolution_bitcast_fusion.2
  666.7 4.7 collective-permute-done.1
  678.0 2.8 multiply_reduce_fusion.4
  690.5 9.2 all-to-all-start.8
  699.8 5.4 fusion.263
  705.3 4.1 fusion.345
  709.4 4.4 all-to-all-done.8
  713.8 5.9 add_convert_fusion.1
  723.1 6.1 all-to-all-start.9
  729.2 2.9 fusion.340
  753.6 2.4 multiply_reduce_fusion.11
  766.3 2.3 convert_element_type.471
  768.7 4.1 multiply_reduce_fusion.12
  774.3 5.7 fusion.97
  798.4 9.6 all-to-all-start.10
  808.0 5.3 fusion.261
  813.3 8.7 all-to-all-done.10
  822.0 10.3 add_convert_fusion
  835.8 5.9 all-to-all-start.11
  841.9 5.4 fusion.343
  874.9 2.9 add_bitcast_fusion.1
  877.9 3.8 copy.414
  881.8 6.6 add_bitcast_fusion
  888.4 10.3 copy.411
  898.8 8.5 fusion.4
  907.3 11.6 fusion.1
  921.1 280.2 %all-reduce.5 = (f32[1,2,768]{2,1,0:T(2,128)S(1)}, f32[1,2,768]{2,1,0:T(2,128)S(1)}) all-reduce(f32[1,2,768]{2,1,0:T(2,128)S(1)} %fusion.442, f32[1,2,768]{2,1,0:T(2,128)S(1)} %fusion.444), channel_id=15, replica_groups=mesh['section'=2,'wide'=64] {'wide'}, use_global_device_ids=true, to_apply=%region_74.75.clone | all-reduce | flops 3072 | bytes 24576
  1205.4 273.7 %all-reduce.9.cloned.1.call-done = (f32[1,768,2304]{2,0,1:T(1,128)}, f32[1,768,768]{2,0,1:T(1,128)}, f32[1,768,32]{2,0,1:T(1,128)}) async-done(((f32[1,768,2304]{2,0,1:T(1,128)}, f32[1,768,768]{2,0,1:T(1,128)}, f32[1,768,32]{2,0,1:T(1,128)}), (f32[1,768,2304]{2,0,1:T(1,128)}, f32[1,768,768]{2,0,1:T(1,128)}, f32[1,768,32]{2,0,1:T(1,128)})) %all-reduce.9.cloned.1.call-update) | async-done | bytes 9535504
  (548 shorter events, 301.1 us)
Async XLA Ops:
  7.2 351.0 %copy-start = (bf16[1,1,768,1536]{3,2,1,0:T(8,128)(2,1)S(1)}, bf16[1,1,768,1536]{3,2,1,0:T(8,128)(2,1)}, u32[]{:S(2)}) copy-start(bf16[1,1,768,1536]{3,2,1,0:T(8,128)(2,1)} %param.15) | copy-start | bytes 7077892
  7.2 182.8 %all-gather.5.cloned.1.call-start = ((), (), s32[]{:S(2)}) async-start(), calls=%async_computation.13 | async-start | bytes 2396160 | tf_op jit(solution)/shard_map/all_gather | solution.py:53
  8.8 219.4 %all-gather.3.cloned.1.call-start = ((), (), s32[]{:S(2)}) async-start(), calls=%async_computation.12 | async-start | bytes 7188480 | tf_op jit(solution)/shard_map/all_gather | solution.py:52
  179.5 10.5 copy-start.116
  184.1 336.9 %copy-start.43 = (f32[768]{0:T(1024)}, f32[768]{0:T(1024)S(1)}, u32[]{:S(2)}) copy-start(f32[768]{0:T(1024)S(1)} %get-tuple-element.39) | copy-start | bytes 9220
  189.4 201.7 %copy-start.51 = (s32[8,128]{1,0:T(8,128)}, s32[8,128]{1,0:T(8,128)S(1)}, u32[]{:S(2)}) copy-start(s32[8,128]{1,0:T(8,128)S(1)} %fusion.445) | copy-start | bytes 12292
  253.0 105.1 %all-to-all-start = ((bf16[64,8,768]{2,1,0:T(8,128)(2,1)}), bf16[64,8,768]{2,1,0:T(8,128)(2,1)}, u32[]{:S(2)}, u32[]{:S(2)}) async-start(bf16[64,8,768]{2,1,0:T(8,128)(2,1)} %bitcast.500), calls=%async_computation | async-start | bytes 1572864 | tf_op jit(solution)/shard_map/all_to_all | solution.py:104
  371.6 19.5 %all-to-all-start.1 = ((bf16[64,8,768]{2,1,0:T(8,128)(2,1)}), bf16[64,8,768]{2,1,0:T(8,128)(2,1)}, u32[]{:S(2)}, u32[]{:S(2)}) async-start(bf16[64,8,768]{2,1,0:T(8,128)(2,1)} %fusion.191), calls=%async_computation.1 | async-start | bytes 1572864 | tf_op jit(solution)/shard_map/all_to_all | solution.py:110
  398.7 7.6 collective-permute-start
  420.6 6.5 copy-start.60
  432.4 19.7 %all-to-all-start.2 = ((bf16[64,8,768]{2,1,0:T(8,128)(2,1)}), bf16[64,8,768]{2,1,0:T(8,128)(2,1)}, u32[]{:S(2)}, u32[]{:S(2)}) async-start(bf16[64,8,768]{2,1,0:T(8,128)(2,1)} %bitcast.501), calls=%async_computation.2 | async-start | bytes 1572864 | tf_op jit(solution)/shard_map/all_to_all | solution.py:104
  465.7 24.4 %all-to-all-start.3 = ((bf16[64,8,768]{2,1,0:T(8,128)(2,1)}), bf16[64,8,768]{2,1,0:T(8,128)(2,1)}, u32[]{:S(2)}, u32[]{:S(2)}) async-start(bf16[64,8,768]{2,1,0:T(8,128)(2,1)} %fusion.196), calls=%async_computation.3 | async-start | bytes 1572864 | tf_op jit(solution)/shard_map/all_to_all | solution.py:110
  509.6 9.0 copy-start.49
  509.6 9.0 collective-permute-start.2
  531.6 11.8 copy-start.53
  533.5 5.5 copy-start.118
  533.5 5.5 copy-start.120
  533.5 6.7 copy-start.61
  544.6 12.8 copy-start.87
  545.5 22.5 %all-to-all-start.6 = ((bf16[64,8,768]{2,1,0:T(8,128)(2,1)}), bf16[64,8,768]{2,1,0:T(8,128)(2,1)}, u32[]{:S(2)}, u32[]{:S(2)}) async-start(bf16[64,8,768]{2,1,0:T(8,128)(2,1)} %bitcast.499), calls=%async_computation.6 | async-start | bytes 1572864 | tf_op jit(solution)/shard_map/all_to_all | solution.py:104
  559.3 34.3 %copy-start.114 = (f32[64]{0:T(128)}, f32[64]{0:T(128)S(1)}, u32[]{:S(2)}) copy-start(f32[64]{0:T(128)S(1)} %reduce_max.59) | copy-start | bytes 772
  570.0 23.7 %all-to-all-start.4 = ((bf16[64,8,768]{2,1,0:T(8,128)(2,1)}), bf16[64,8,768]{2,1,0:T(8,128)(2,1)}, u32[]{:S(2)}, u32[]{:S(2)}) async-start(bf16[64,8,768]{2,1,0:T(8,128)(2,1)} %bitcast.502), calls=%async_computation.4 | async-start | bytes 1572864 | tf_op jit(solution)/shard_map/all_to_all | solution.py:175
  603.0 24.9 %all-to-all-start.5 = ((bf16[64,8,768]{2,1,0:T(8,128)(2,1)}), bf16[64,8,768]{2,1,0:T(8,128)(2,1)}, u32[]{:S(2)}, u32[]{:S(2)}) async-start(bf16[64,8,768]{2,1,0:T(8,128)(2,1)} %fusion.206), calls=%async_computation.5 | async-start | bytes 1572864 | tf_op jit(solution)/shard_map/all_to_all | solution.py:185
  612.1 6.8 copy-start.127
  612.1 6.8 copy-start.135
  618.9 18.1 %copy-start.52 = (s32[8,128]{1,0:T(8,128)S(1)}, s32[8,128]{1,0:T(8,128)}, u32[]{:S(2)}) copy-start(s32[8,128]{1,0:T(8,128)} %copy-done.51) | copy-start | bytes 12292
  627.9 36.4 %all-to-all-start.7 = ((bf16[64,8,768]{2,1,0:T(8,128)(2,1)}), bf16[64,8,768]{2,1,0:T(8,128)(2,1)}, u32[]{:S(2)}, u32[]{:S(2)}) async-start(bf16[64,8,768]{2,1,0:T(8,128)(2,1)} %fusion.201), calls=%async_computation.7 | async-start | bytes 1572864 | tf_op jit(solution)/shard_map/all_to_all | solution.py:110
  663.0 8.4 collective-permute-start.1
  690.5 23.3 %all-to-all-start.8 = ((bf16[64,8,768]{2,1,0:T(8,128)(2,1)}), bf16[64,8,768]{2,1,0:T(8,128)(2,1)}, u32[]{:S(2)}, u32[]{:S(2)}) async-start(bf16[64,8,768]{2,1,0:T(8,128)(2,1)} %bitcast.503), calls=%async_computation.8 | async-start | bytes 1572864 | tf_op jit(solution)/shard_map/all_to_all | solution.py:175
  699.7 5.5 copy-start.5
  699.8 5.4 copy-start.10
  723.1 22.8 %all-to-all-start.9 = ((bf16[64,8,768]{2,1,0:T(8,128)(2,1)}), bf16[64,8,768]{2,1,0:T(8,128)(2,1)}, u32[]{:S(2)}, u32[]{:S(2)}) async-start(bf16[64,8,768]{2,1,0:T(8,128)(2,1)} %fusion.209), calls=%async_computation.9 | async-start | bytes 1572864 | tf_op jit(solution)/shard_map/all_to_all | solution.py:185
  768.7 5.6 copy-start.134
  773.0 7.0 copy-start.46
  773.0 8.3 collective-permute-start.3
  798.4 23.7 %all-to-all-start.10 = ((bf16[64,8,768]{2,1,0:T(8,128)(2,1)}), bf16[64,8,768]{2,1,0:T(8,128)(2,1)}, u32[]{:S(2)}, u32[]{:S(2)}) async-start(bf16[64,8,768]{2,1,0:T(8,128)(2,1)} %bitcast.504), calls=%async_computation.10 | async-start | bytes 1572864 | tf_op jit(solution)/shard_map/all_to_all | solution.py:175
  835.8 19.9 %all-to-all-start.11 = ((bf16[64,8,768]{2,1,0:T(8,128)(2,1)}), bf16[64,8,768]{2,1,0:T(8,128)(2,1)}, u32[]{:S(2)}, u32[]{:S(2)}) async-start(bf16[64,8,768]{2,1,0:T(8,128)(2,1)} %fusion.212), calls=%async_computation.11 | async-start | bytes 1572864 | tf_op jit(solution)/shard_map/all_to_all | solution.py:185
  841.6 637.4 %all-reduce.9.cloned.1.call-start = ((), (), s32[]{:S(2)}) async-start(), calls=%async_computation.14 | async-start | bytes 19660800
  841.7 5.6 copy-start.92
  841.7 6.2 copy-start.91
  841.7 6.8 copy-start.96
  841.7 7.3 copy-start.95
  841.7 7.9 copy-start.22
  841.7 7.9 copy-start.40
  841.8 7.9 copy-start.42
  841.8 9.9 copy-start.105
  841.8 9.9 copy-start.106
  841.8 9.9 copy-start.123
  841.8 9.9 copy-start.88
  841.8 9.9 copy-start.89
  841.8 10.5 copy-start.30
  841.8 10.5 copy-start.33
  841.8 10.5 copy-start.48
  857.2 7.0 copy-start.124
  898.7 8.5 copy-start.129
  898.8 8.5 copy-start.136
  907.3 11.7 copy-start.94
  907.3 11.7 copy-start.93
  907.3 11.7 copy-start.2
  907.3 11.7 copy-start.81
  907.3 11.7 copy-start.86
  919.0 285.7 %copy-start.45 = (bf16[1,1,64,768]{3,2,1,0:T(8,128)(2,1)S(1)}, bf16[1,1,64,768]{3,2,1,0:T(8,128)(2,1)}, u32[]{:S(2)}) copy-start(bf16[1,1,64,768]{3,2,1,0:T(8,128)(2,1)} %get-tuple-element.90) | copy-start | bytes 294916
  919.0 285.7 %copy-start.47 = (bf16[64,768]{1,0:T(8,128)(2,1)S(1)}, bf16[64,768]{1,0:T(8,128)(2,1)}, u32[]{:S(2)}) copy-start(bf16[64,768]{1,0:T(8,128)(2,1)} %copy-done.46) | copy-start | bytes 294916
  919.0 285.7 %copy-start.50 = (bf16[64,768]{1,0:T(8,128)(2,1)S(1)}, bf16[64,768]{1,0:T(8,128)(2,1)}, u32[]{:S(2)}) copy-start(bf16[64,768]{1,0:T(8,128)(2,1)} %copy-done.49) | copy-start | bytes 294916
  (92 other events, 239.4 us)
Sparse Core Ops, SparseCore 0:
  10.3 106.7 all-gather.4
  119.4 108.6 all-gather.2
  898.9 580.1 all-reduce.8
where the time goes:
time: 1510 us; the launch traced here: 1490 us
  blocking collectives  531 us (35%)
  waiting for transfers between devices  346 us (23%)
  matrix products  224 us (15%)
  local copies, waits for them, and re-layouts  172 us (11%)
  other arithmetic  100 us (7%)
  starting transfers between devices  99.9 us (7%)
  between operations  16.8 us (1%)
    unnamed x1, blocking collectives  280 us
    unnamed x4, waiting for transfers between devices  274 us
    all_gather x1, blocking collectives, fetch_dense(): lax.all_gather(route_weight, 'wide', axis=1, tiled=True)  88.6 us
    all_gather x1, blocking collectives, fetch_dense(): lax.all_gather(norm_shifts, 'wide', axis=2, tiled=True)  84.9 us
    all_gather x1, blocking collectives, fetch_dense(): lax.all_gather(norm_gains, 'wide', axis=2, tiled=True)  77.6 us
    unnamed x290, local copies, waits for them, and re-layouts  44.5 us
    all_gather x1, waiting for transfers between devices, fetch_dense(): lax.all_gather(qkv_weight, 'wide', axis=1, tiled=True)  36.3 us
  transfers between devices with their start and end apart: 19, of which 11 were waited for; matrix products, arithmetic and copies ran while one was open for 14% of the time, Pallas kernels for 0%

commit v1 on v0

v1 whole, which is shorter than its diff:
```python
from functools import partial

import jax
import jax.numpy as jnp
from jax import lax
from jax.experimental import pallas as pl
from jax.experimental.pallas import tpu as pltpu
from jax.sharding import PartitionSpec as P

HEADS = 12
HD = 64
EPSILON = 1e-06
PRECISE = lax.Precision.HIGHEST


MESH = pl.DeviceIdType.MESH
BLOCK = 304
SLOTS = 16


def place():
    section = lax.axis_index("section")
    wide = lax.axis_index("wide")
    return section, wide // 32, (wide // 8) % 4, (wide // 2) % 4, wide % 2


def wide_of(x, y, z, core):
    return ((x * 4 + y) * 4 + z) * 2 + core


def greet(section, peers):
    barrier = pltpu.get_barrier_semaphore()
    for peer in peers:
        pl.semaphore_signal(barrier, inc=1, device_id=(section, peer), device_id_type=MESH)
    pl.semaphore_wait(barrier, len(peers))


def remote(source, target, send_sem, recv_sem, device):
    return pltpu.make_async_remote_copy(
        src_ref=source,
        dst_ref=target,
        send_sem=send_sem,
        recv_sem=recv_sem,
        device_id=device,
        device_id_type=MESH,
    )


def flow_peer(fx, x, first, second, core):
    return (1 - fx) * wide_of(x, second, first, core) + fx * wide_of(x, first, second, core)


def flow_axes(fx, y, z):
    return (1 - fx) * z + fx * y, (1 - fx) * y + fx * z


def gather_peers(x, y, z, core):
    return (
        [wide_of(1 - x, y, z, core), wide_of(x, y, z, 1 - core)]
        + [wide_of(x, y, (z + k) % 4, core) for k in (1, 2, 3)]
        + [wide_of(x, (y + k) % 4, z, core) for k in (1, 2, 3)]
    )


def gather_kernel(block_ref, full_ref, send_sem, recv_sem, local_sem):
    section, x, y, z, core = place()
    greet(section, gather_peers(x, y, z, core))
    flows = []
    for fx in (x, 1 - x):
        first, second = flow_axes(fx, y, z)
        flows.append((fx, first, second, core * 32 + fx * 16 + 4 * second))
    started = []

    def send(source, target, number, device):
        copy = remote(source, target, send_sem.at[number], recv_sem.at[number], (section, device))
        copy.start()
        started.append(copy)
        return copy

    fx, first, second, base = flows[0]
    mine = base + first
    across = send(block_ref, full_ref.at[mine], 0, wide_of(1 - x, y, z, core))
    keep = pltpu.make_async_copy(block_ref, full_ref.at[mine], local_sem.at[0])
    keep.start()
    near = [[], []]
    for k in (1, 3, 2):
        near[0].append(
            send(block_ref, full_ref.at[mine], k, flow_peer(fx, x, (first + k) % 4, second, core))
        )
    across.wait_recv()
    fx, first, second, base = flows[1]
    theirs = base + first
    for k in (1, 3, 2):
        near[1].append(
            send(
                full_ref.at[theirs],
                full_ref.at[theirs],
                3 + k,
                flow_peer(fx, x, (first + k) % 4, second, core),
            )
        )
    keep.wait()
    sibling = wide_of(x, y, z, 1 - core)
    ring = [None, None]
    pair = []
    number = 7
    for f in (0, 1):
        fx, first, second, base = flows[f]
        for copy in near[f]:
            copy.wait_recv()
        group = full_ref.at[pl.ds(base, 4)]
        ring[f] = []
        for k in (1, 3):
            ring[f].append(
                send(group, group, number, flow_peer(fx, x, first, (second + k) % 4, core))
            )
            number += 1
        pair.append(send(group, group, number, sibling))
        number += 1
    half = [[], []]
    for turn in (0, 1):
        for f in (0, 1):
            fx, first, second, base = flows[f]
            k = (1, 3)[turn]
            ring[f][turn].wait_recv()
            origin = core * 32 + fx * 16 + 4 * ((second + 4 - k) % 4)
            piece = full_ref.at[pl.ds(origin + 2 * turn, 2)]
            half[f].append(
                send(piece, piece, number, flow_peer(fx, x, first, (second + k) % 4, core))
            )
            number += 1
            group = full_ref.at[pl.ds(origin, 4)]
            pair.append(send(group, group, number, sibling))
            number += 1
    for turn in (0, 1):
        for f in (0, 1):
            fx, first, second, base = flows[f]
            half[f][turn].wait_recv()
            origin = core * 32 + fx * 16 + 4 * ((second + 2) % 4)
            piece = full_ref.at[pl.ds(origin + 2 * turn, 2)]
            pair.append(send(piece, piece, number, sibling))
            number += 1
    for copy in pair:
        copy.wait_recv()
    for copy in started:
        copy.wait_send()


def gather_blocks(block):
    return pl.pallas_call(
        gather_kernel,
        out_shape=jax.ShapeDtypeStruct((64, BLOCK, 128), jnp.bfloat16),
        in_specs=[pl.BlockSpec(memory_space=pl.ANY)],
        out_specs=pl.BlockSpec(memory_space=pl.ANY),
        scratch_shapes=[
            pltpu.SemaphoreType.DMA((32,)),
            pltpu.SemaphoreType.DMA((32,)),
            pltpu.SemaphoreType.DMA((1,)),
        ],
        compiler_params=pltpu.CompilerParams(collective_id=0, has_side_effects=True),
        name="gather_blocks",
    )(block)


def scatter_kernel(
    parts_ref, out_ref, own, pair_land, ring_land, ring_send, near_land, near_send, last,
    send_sem, recv_sem, local_sem,
):
    section, x, y, z, core = place()
    greet(section, gather_peers(x, y, z, core))
    sibling = wide_of(x, y, z, 1 - core)
    started = []

    def send(source, target, number, device):
        copy = remote(source, target, send_sem.at[number], recv_sem.at[number], (section, device))
        copy.start()
        started.append(copy)
        return copy

    order = []
    for k in (2, 1, 3, 0):
        for f in (0, 1):
            order.append((k, f))
    axes = []
    for f in (0, 1):
        fx = x if f == 0 else 1 - x
        first, second = flow_axes(fx, y, z)
        axes.append((fx, first, second))
    pair, kept = {}, {}
    number = 0
    for k, f in order:
        fx, first, second = axes[f]
        place_of = (second + k) % 4
        pair[k, f] = send(
            parts_ref.at[1 - core, fx, place_of], pair_land.at[k, f], number, sibling
        )
        kept[k, f] = pltpu.make_async_copy(
            parts_ref.at[core, fx, place_of], own.at[k, f], local_sem.at[number]
        )
        kept[k, f].start()
        number += 1

    def total(k, f, lo, hi):
        return own[k, f, lo:hi].astype(jnp.float32) + pair_land[k, f, lo:hi].astype(jnp.float32)

    relay = {}
    for f in (0, 1):
        fx, first, second = axes[f]
        pair[2, f].wait_recv()
        kept[2, f].wait()
        ring_send[2, f] = total(2, f, 0, 4).astype(jnp.bfloat16)
        for turn, k in ((0, 1), (1, 3)):
            relay[turn, f] = send(
                ring_send.at[2, f, pl.ds(2 * turn, 2)],
                ring_land.at[2, f, pl.ds(2 * turn, 2)],
                number,
                flow_peer(fx, x, first, (second + k) % 4, core),
            )
            number += 1
    ring = {}
    for turn, k in ((0, 1), (1, 3)):
        for f in (0, 1):
            fx, first, second = axes[f]
            pair[k, f].wait_recv()
            kept[k, f].wait()
            relay[turn, f].wait_recv()
            lo = 2 * turn
            rest = 2 - lo
            ring_send[turn, f, lo : lo + 2] = (
                total(k, f, lo, lo + 2) + ring_land[2, f, lo : lo + 2].astype(jnp.float32)
            ).astype(jnp.bfloat16)
            ring_send[turn, f, rest : rest + 2] = total(k, f, rest, rest + 2).astype(jnp.bfloat16)
            ring[turn, f] = send(
                ring_send.at[turn, f],
                ring_land.at[turn, f],
                number,
                flow_peer(fx, x, first, (second + k) % 4, core),
            )
            number += 1
    near = {}
    for f in (0, 1):
        pair[0, f].wait_recv()
        kept[0, f].wait()
    for f in (1, 0):
        fx, first, second = axes[f]
        for turn in (0, 1):
            ring[turn, f].wait_recv()
        near_send[f] = (
            total(0, f, 0, 4)
            + ring_land[0, f].astype(jnp.float32)
            + ring_land[1, f].astype(jnp.float32)
        ).astype(jnp.bfloat16)
        for k in (1, 3, 2):
            near[k, f] = send(
                near_send.at[f, (first + k) % 4],
                near_land.at[f, k],
                number,
                flow_peer(fx, x, (first + k) % 4, second, core),
            )
            number += 1

    def settled(f):
        fx, first, second = axes[f]
        value = near_send[f, first].astype(jnp.float32)
        for k in (1, 3, 2):
            near[k, f].wait_recv()
            value = value + near_land[f, k].astype(jnp.float32)
        return value

    last[0] = settled(1).astype(jnp.bfloat16)
    final = send(last.at[0], last.at[1], number, wide_of(1 - x, y, z, core))
    here = settled(0)
    final.wait_recv()
    out_ref[...] = here + last[1].astype(jnp.float32)
    for copy in started:
        copy.wait_send()


def scatter_blocks(parts):
    return pl.pallas_call(
        scatter_kernel,
        out_shape=jax.ShapeDtypeStruct((BLOCK, 128), jnp.float32),
        in_specs=[pl.BlockSpec(memory_space=pl.ANY)],
        out_specs=pl.BlockSpec(memory_space=pltpu.VMEM),
        scratch_shapes=[
            pltpu.VMEM((4, 2, 4, BLOCK, 128), jnp.bfloat16),
            pltpu.VMEM((4, 2, 4, BLOCK, 128), jnp.bfloat16),
            pltpu.VMEM((3, 2, 4, BLOCK, 128), jnp.bfloat16),
            pltpu.VMEM((3, 2, 4, BLOCK, 128), jnp.bfloat16),
            pltpu.VMEM((2, 4, BLOCK, 128), jnp.bfloat16),
            pltpu.VMEM((2, 4, BLOCK, 128), jnp.bfloat16),
            pltpu.VMEM((2, BLOCK, 128), jnp.bfloat16),
            pltpu.SemaphoreType.DMA((32,)),
            pltpu.SemaphoreType.DMA((32,)),
            pltpu.SemaphoreType.DMA((8,)),
        ],
        compiler_params=pltpu.CompilerParams(
            collective_id=1, has_side_effects=True, vmem_limit_bytes=40 * 2**20
        ),
        name="scatter_blocks",
    )(parts)


def exchange_peers(x, y, z, core):
    peers = [wide_of(x, y, z, 1 - core)]
    for dx in (0, 1):
        for dy in range(4):
            for dz in range(4):
                if dx + dy + dz:
                    peers.append(wide_of((x + dx) % 2, (y + dy) % 4, (z + dz) % 4, core))
    return peers


GROUPS = [(0, 0), (1, 0), (0, 1), (1, 1), (0, 3), (1, 3), (0, 2), (1, 2)]


def dispatch_kernel(rows_ref, got_ref, send_sem, recv_sem, pair_send, pair_recv, local_sem):
    section, x, y, z, core = place()
    greet(section, exchange_peers(x, y, z, core))
    here = x * 16 + y * 4 + z
    keep = pltpu.make_async_copy(rows_ref.at[here], got_ref.at[core, here], local_sem.at[0])
    keep.start()
    copies = {}
    for number, (dx, dy) in enumerate(GROUPS):
        for dz in (0, 1, 3, 2):
            if dx + dy + dz == 0:
                continue
            tx, ty, tz = (x + dx) % 2, (y + dy) % 4, (z + dz) % 4
            copies[number, dz] = remote(
                rows_ref.at[tx * 16 + ty * 4 + tz],
                got_ref.at[core, here],
                send_sem.at[4 * number + dz],
                recv_sem.at[4 * number + dz],
                (section, wide_of(tx, ty, tz, core)),
            )
            copies[number, dz].start()
    keep.wait()
    pairs = []
    for number, (dx, dy) in enumerate(GROUPS):
        for dz in (0, 1, 3, 2):
            if dx + dy + dz:
                copies[number, dz].wait_recv()
        first = ((x + dx) % 2) * 16 + ((y + 4 - dy) % 4) * 4
        piece = got_ref.at[core, pl.ds(first, 4)]
        pair = remote(
            piece,
            piece,
            pair_send.at[number],
            pair_recv.at[number],
            (section, wide_of(x, y, z, 1 - core)),
        )
        pair.start()
        pairs.append(pair)
    for pair in pairs:
        pair.wait()
    for copy in copies.values():
        copy.wait_send()


def dispatch(rows):
    return pl.pallas_call(
        dispatch_kernel,
        out_shape=jax.ShapeDtypeStruct((2, 32, SLOTS, 768), jnp.bfloat16),
        in_specs=[pl.BlockSpec(memory_space=pl.ANY)],
        out_specs=pl.BlockSpec(memory_space=pl.ANY),
        scratch_shapes=[
            pltpu.SemaphoreType.DMA((32,)),
            pltpu.SemaphoreType.DMA((32,)),
            pltpu.SemaphoreType.DMA((8,)),
            pltpu.SemaphoreType.DMA((8,)),
            pltpu.SemaphoreType.DMA((1,)),
        ],
        compiler_params=pltpu.CompilerParams(collective_id=2, has_side_effects=True),
        name="dispatch",
    )(rows)


def collect_kernel(
    part_ref, got_ref, own, land, summed, send_sem, recv_sem, pair_send, pair_recv, local_sem
):
    section, x, y, z, core = place()
    greet(section, exchange_peers(x, y, z, core))
    here = x * 16 + y * 4 + z
    pairs = []
    keeps = []
    firsts = []
    for number, (dx, dy) in enumerate(GROUPS):
        first = ((x + dx) % 2) * 16 + ((y + dy) % 4) * 4
        firsts.append(first)
        pair = remote(
            part_ref.at[1 - core, pl.ds(first, 4)],
            land.at[number],
            pair_send.at[number],
            pair_recv.at[number],
            (section, wide_of(x, y, z, 1 - core)),
        )
        pair.start()
        pairs.append(pair)
        keep = pltpu.make_async_copy(
            part_ref.at[core, pl.ds(first, 4)], own.at[number], local_sem.at[number]
        )
        keep.start()
        keeps.append(keep)
    copies = {}
    for number, (dx, dy) in enumerate(GROUPS):
        pairs[number].wait_recv()
        keeps[number].wait()
        summed[number] = (
            own[number].astype(jnp.float32) + land[number].astype(jnp.float32)
        ).astype(jnp.bfloat16)
        for dz in (0, 1, 3, 2):
            tx, ty, tz = (x + dx) % 2, (y + dy) % 4, (z + dz) % 4
            if dx + dy + dz == 0:
                last = pltpu.make_async_copy(
                    summed.at[number, tz], got_ref.at[here], local_sem.at[8]
                )
                last.start()
                continue
            copies[number, dz] = remote(
                summed.at[number, tz],
                got_ref.at[here],
                send_sem.at[4 * number + dz],
                recv_sem.at[4 * number + dz],
                (section, wide_of(tx, ty, tz, core)),
            )
            copies[number, dz].start()
    last.wait()
    for copy in copies.values():
        copy.wait()
    for pair in pairs:
        pair.wait_send()


def collect(part):
    return pl.pallas_call(
        collect_kernel,
        out_shape=jax.ShapeDtypeStruct((32, SLOTS, 768), jnp.bfloat16),
        in_specs=[pl.BlockSpec(memory_space=pl.ANY)],
        out_specs=pl.BlockSpec(memory_space=pl.ANY),
        scratch_shapes=[
            pltpu.VMEM((8, 4, SLOTS, 768), jnp.bfloat16),
            pltpu.VMEM((8, 4, SLOTS, 768), jnp.bfloat16),
            pltpu.VMEM((8, 4, SLOTS, 768), jnp.bfloat16),
            pltpu.SemaphoreType.DMA((32,)),
            pltpu.SemaphoreType.DMA((32,)),
            pltpu.SemaphoreType.DMA((8,)),
            pltpu.SemaphoreType.DMA((8,)),
            pltpu.SemaphoreType.DMA((9,)),
        ],
        compiler_params=pltpu.CompilerParams(
            collective_id=3, has_side_effects=True, vmem_limit_bytes=32 * 2**20
        ),
        name="collect",
    )(part)


def shifted(value, axis, steps):
    count = lax.axis_size(axis)
    initial, last = (max(0, -steps), min(count, count - steps))
    return lax.ppermute(value, axis, [(source, source + steps) for source in range(initial, last)])


def normalize(values, gain_row, shift_row):
    centered = values - jnp.mean(values, axis=-1, keepdims=True)
    inverse = lax.rsqrt(jnp.mean(centered * centered, axis=-1, keepdims=True) + EPSILON)
    unit_rows = centered * inverse
    return (unit_rows * gain_row + shift_row, unit_rows, inverse)


def normalize_back(grad_rows, unit_rows, inverse, gain_row):
    scaled = grad_rows * gain_row
    inner = (
        scaled
        - jnp.mean(scaled, axis=-1, keepdims=True)
        - unit_rows * jnp.mean(scaled * unit_rows, axis=-1, keepdims=True)
    )
    return (inner * inverse, jnp.sum(grad_rows * unit_rows, axis=0), jnp.sum(grad_rows, axis=0))


def pack_block(qkv_weight, attn_weight, route_weight, norm_gains, norm_shifts):
    wide = jnp.concatenate([qkv_weight[0], attn_weight[0]], axis=1)
    wide = wide.reshape(12, 24, 128).transpose(1, 0, 2).reshape(288, 128)
    small = jnp.concatenate([norm_gains[0], norm_shifts[0]], axis=0).reshape(48)
    extra = jnp.concatenate([route_weight.reshape(384), small, jnp.zeros((1616,), jnp.bfloat16)])
    return jnp.concatenate([wide, extra.reshape(16, 128)], axis=0)


def by_place(blocks):
    parts = blocks.reshape(2, 2, 4, 4, *blocks.shape[1:])
    low, high = parts[:, 0], parts[:, 1].swapaxes(1, 2)
    return jnp.moveaxis(jnp.stack([low, high], axis=1), 0, 3).reshape(blocks.shape)


def by_slot(blocks):
    parts = jnp.moveaxis(blocks.reshape(2, 4, 4, 2, *blocks.shape[1:]), 3, 0)
    low, high = parts[:, 0], parts[:, 1].swapaxes(1, 2)
    return jnp.stack([low, high], axis=1)


def fetch_dense(*shards):
    blocks = by_place(gather_blocks(pack_block(*shards)))
    wide = blocks[:, :288].reshape(64, 24, 12, 128).transpose(0, 2, 1, 3).reshape(768, 3072)
    route = blocks[:, 288:291].reshape(768, 32)
    small = blocks[:, 291, :48].reshape(64, 4, 12).transpose(1, 0, 2).reshape(4, 768)
    return wide[:, :2304], wide[:, 2304:], route, small[:2], small[2:]


def share_dense(qkv_grad, attn_grad, route_grad, gain_grad, shift_grad):
    wide = jnp.concatenate([qkv_grad, attn_grad], axis=1).astype(jnp.bfloat16)
    wide = wide.reshape(64, 12, 24, 128).transpose(0, 2, 1, 3).reshape(64, 288, 128)
    small = jnp.concatenate([gain_grad, shift_grad], axis=0).astype(jnp.bfloat16)
    small = small.reshape(4, 64, 12).transpose(1, 0, 2).reshape(64, 48)
    extra = jnp.concatenate(
        [
            route_grad.astype(jnp.bfloat16).reshape(64, 384),
            small,
            jnp.zeros((64, 1616), jnp.bfloat16),
        ],
        axis=1,
    ).reshape(64, 16, 128)
    mine = scatter_blocks(by_slot(jnp.concatenate([wide, extra], axis=1)))
    own = mine[:288].reshape(24, 12, 128).transpose(1, 0, 2).reshape(12, 3072)
    small = mine[291, :48].reshape(4, 12)
    return (
        own[None, :, :2304],
        own[None, :, 2304:],
        mine[288:291].reshape(1, 12, 32),
        small[None, :2],
        small[None, 2:],
    )


def build_slots(route_rows):
    batches, tokens, _ = route_rows.shape
    assigned = route_rows.reshape(batches, 2 * tokens)
    onehot = (assigned[:, :, None] == jnp.arange(32, dtype=jnp.int32)).astype(jnp.int32)
    earlier = jnp.cumsum(onehot, axis=1) - onehot
    position = jnp.sum(earlier * onehot, axis=2)
    number = (assigned * 8 + position).reshape(batches, tokens, 2)
    slots = number[:, None] == jnp.arange(256, dtype=jnp.int32)[None, :, None, None]
    return slots.transpose(0, 1, 3, 2).astype(jnp.bfloat16)


def to_experts(slot_map, rows):
    sent = jnp.einsum("bskt,bktd->bsd", slot_map, rows, preferred_element_type=jnp.float32)
    sent = sent.astype(jnp.bfloat16).reshape(2, 32, 8, 768)
    return sent.transpose(1, 0, 2, 3).reshape(32, SLOTS, 768)


def from_experts(slot_map, got):
    got = got.reshape(32, 2, 8, 768).transpose(1, 0, 2, 3).reshape(2, 256, 768)
    return jnp.einsum("bskt,bsd->bktd", slot_map, got, preferred_element_type=jnp.float32)


def forward_layer(stream, dense_now, weight_in, weight_out, slot_map, chosen):
    weight_qkv, weight_attn, weight_route, gain_rows, shift_rows = dense_now
    gain_rows, shift_rows = gain_rows.astype(jnp.float32), shift_rows.astype(jnp.float32)
    batches, tokens, width = stream.shape
    scaling = HD ** (-0.5)
    normed_one, unit_one, inverse_one = normalize(stream, gain_rows[0], shift_rows[0])
    entering = normed_one.astype(jnp.bfloat16)
    projected = jnp.einsum(
        "btd,de->bte", entering, weight_qkv, preferred_element_type=jnp.float32
    ).astype(jnp.bfloat16)
    heads = projected.reshape(batches, tokens, 3, HEADS, HD)
    scores = (
        jnp.einsum(
            "bqhd,bkhd->bhqk", heads[:, :, 0], heads[:, :, 1], preferred_element_type=jnp.float32
        )
        * scaling
    )
    probs = jax.nn.softmax(scores, axis=-1)
    attended = jnp.einsum(
        "bhqk,bkhd->bqhd",
        probs.astype(jnp.bfloat16),
        heads[:, :, 2],
        preferred_element_type=jnp.float32,
    )
    attended = attended.astype(jnp.bfloat16).reshape(batches, tokens, width)
    hidden = stream + jnp.einsum(
        "btd,de->bte", attended, weight_attn, preferred_element_type=jnp.float32
    )
    normed_two, unit_two, inverse_two = normalize(hidden, gain_rows[1], shift_rows[1])
    leaving = normed_two.astype(jnp.bfloat16)
    logits = jnp.einsum(
        "btd,de->bte", leaving, weight_route, preferred_element_type=jnp.float32
    )
    gate_rows = jax.nn.softmax(jnp.sum(chosen * logits[:, :, None, :], axis=3), axis=-1)
    sending = to_experts(slot_map, jnp.stack([leaving, leaving], axis=1))
    arrived = dispatch(sending).reshape(1024, 768)
    raised = jnp.dot(arrived, weight_in, preferred_element_type=jnp.float32)
    activated = jax.nn.gelu(raised, approximate=False).astype(jnp.bfloat16)
    part = jnp.dot(activated, weight_out, preferred_element_type=jnp.float32)
    returned = collect(part.astype(jnp.bfloat16).reshape(2, 32, SLOTS, 768))
    combined = from_experts(slot_map, returned)
    output = hidden + jnp.sum(gate_rows.swapaxes(1, 2)[:, :, :, None] * combined, axis=1)
    stored = (
        unit_one, inverse_one, entering, heads, probs, attended, unit_two, inverse_two, leaving,
        gate_rows, combined, arrived, raised,
    )
    return output, stored


def backward_layer(grad_out, stored, dense_now, weight_in, weight_out, slot_map, chosen):
    weight_qkv, weight_attn, weight_route, gain_rows, shift_rows = dense_now
    gain_rows, shift_rows = gain_rows.astype(jnp.float32), shift_rows.astype(jnp.float32)
    (
        unit_one, inverse_one, entering, heads, probs, attended, unit_two, inverse_two, leaving,
        gate_rows, combined, arrived, raised,
    ) = stored
    batches, tokens, width = grad_out.shape
    scaling = HD ** (-0.5)
    gate_grad = jnp.sum(combined * grad_out[:, None], axis=3).swapaxes(1, 2)
    logit_pair = gate_rows * (gate_grad - jnp.sum(gate_rows * gate_grad, axis=2, keepdims=True))
    logit_grad = jnp.sum(chosen * logit_pair[:, :, :, None], axis=2)
    route_grad = jnp.einsum(
        "btd,bte->de", leaving.astype(jnp.float32), logit_grad, precision=PRECISE
    )
    leaving_grad = jnp.einsum(
        "bte,de->btd", logit_grad, weight_route.astype(jnp.float32), precision=PRECISE
    )
    part_grad = (gate_rows.swapaxes(1, 2)[:, :, :, None] * grad_out[:, None]).astype(jnp.bfloat16)
    incoming = dispatch(to_experts(slot_map, part_grad)).reshape(1024, 768)
    activated = jax.nn.gelu(raised, approximate=False).astype(jnp.bfloat16)
    out_grad = jnp.einsum("nf,nd->fd", activated, incoming, preferred_element_type=jnp.float32)
    act_grad = jnp.einsum("nd,fd->nf", incoming, weight_out, preferred_element_type=jnp.float32)
    gelu_back = jax.vjp(partial(jax.nn.gelu, approximate=False), raised)[1]
    raised_grad = gelu_back(act_grad)[0].astype(jnp.bfloat16)
    in_grad = jnp.einsum("nd,nf->df", arrived, raised_grad, preferred_element_type=jnp.float32)
    row_grad = jnp.einsum("nf,df->nd", raised_grad, weight_in, preferred_element_type=jnp.float32)
    back = collect(row_grad.astype(jnp.bfloat16).reshape(2, 32, SLOTS, 768))
    leaving_grad = leaving_grad + jnp.sum(from_experts(slot_map, back), axis=1)
    normed_grad, gain_two, shift_two = normalize_back(
        leaving_grad, unit_two, inverse_two, gain_rows[1]
    )
    hidden_grad = grad_out + normed_grad
    branch_grad = hidden_grad.astype(jnp.bfloat16)
    attn_grad = jnp.einsum("btd,bte->de", attended, branch_grad, preferred_element_type=jnp.float32)
    attended_grad = jnp.einsum(
        "bte,de->btd", branch_grad, weight_attn, preferred_element_type=jnp.float32
    )
    attended_grad = attended_grad.astype(jnp.bfloat16).reshape(batches, tokens, HEADS, HD)
    queries, keys_in, values_in = heads[:, :, 0], heads[:, :, 1], heads[:, :, 2]
    value_grad = jnp.einsum(
        "bhqk,bqhd->bkhd",
        probs.astype(jnp.bfloat16),
        attended_grad,
        preferred_element_type=jnp.float32,
    )
    prob_grad = jnp.einsum(
        "bqhd,bkhd->bhqk", attended_grad, values_in, preferred_element_type=jnp.float32
    )
    score_grad = (probs * (prob_grad - jnp.sum(probs * prob_grad, axis=-1, keepdims=True))).astype(
        jnp.bfloat16
    )
    query_grad = (
        jnp.einsum("bhqk,bkhd->bqhd", score_grad, keys_in, preferred_element_type=jnp.float32)
        * scaling
    )
    key_grad = (
        jnp.einsum("bhqk,bqhd->bkhd", score_grad, queries, preferred_element_type=jnp.float32)
        * scaling
    )
    projected_grad = (
        jnp.stack([query_grad, key_grad, value_grad], axis=2)
        .reshape(batches, tokens, 3 * width)
        .astype(jnp.bfloat16)
    )
    qkv_grad = jnp.einsum(
        "btd,bte->de", entering, projected_grad, preferred_element_type=jnp.float32
    )
    entering_grad = jnp.einsum(
        "bte,de->btd", projected_grad, weight_qkv, preferred_element_type=jnp.float32
    )
    normed_grad, gain_one, shift_one = normalize_back(
        entering_grad, unit_one, inverse_one, gain_rows[0]
    )
    stream_grad = hidden_grad + normed_grad
    dense_grads = (
        qkv_grad,
        attn_grad,
        route_grad,
        jnp.stack([jnp.sum(gain_one, axis=0), jnp.sum(gain_two, axis=0)]),
        jnp.stack([jnp.sum(shift_one, axis=0), jnp.sum(shift_two, axis=0)]),
    )
    return stream_grad, dense_grads, in_grad, out_grad


def body(
    section_ends,
    qkv_weight,
    attn_weight,
    route_weight,
    norm_gains,
    norm_shifts,
    expert_in,
    expert_out,
    routes,
):
    ends_here = section_ends[0]
    leading = lax.axis_index("section") == 0
    weight_in, weight_out = expert_in[0, 0], expert_out[0, 0]
    dense = fetch_dense(qkv_weight, attn_weight, route_weight, norm_gains, norm_shifts)
    slot_map = build_slots(routes[0])
    chosen = (routes[0][:, :, :, None] == jnp.arange(32, dtype=jnp.int32)).astype(jnp.float32)

    output, _ = forward_layer(
        ends_here.astype(jnp.float32), dense, weight_in, weight_out, slot_map, chosen
    )
    arriving = shifted(output.astype(jnp.bfloat16), "section", 1)
    stream = jnp.where(leading, ends_here, arriving).astype(jnp.float32)
    output, stored = forward_layer(stream, dense, weight_in, weight_out, slot_map, chosen)

    grad_out = ends_here.astype(jnp.float32)
    stream_grad, _, _, _ = backward_layer(
        grad_out, stored, dense, weight_in, weight_out, slot_map, chosen
    )
    arriving = shifted(stream_grad.astype(jnp.bfloat16), "section", -1)
    grad_out = jnp.where(leading, arriving, ends_here).astype(jnp.float32)
    stream_grad, dense_grads, in_grad, out_grad = backward_layer(
        grad_out, stored, dense, weight_in, weight_out, slot_map, chosen
    )
    shares = share_dense(*dense_grads)
    finished = jnp.where(leading, stream_grad, output).astype(jnp.bfloat16)
    return (finished[None], *shares, in_grad[None, None], out_grad[None, None])


def solution(mesh):
    wide_rows, wide_ends = P("section", "wide", None), P("section", None, "wide", None)
    wide_last, experts = P("section", None, "wide"), P("section", "wide", None, None)
    dense = (wide_rows, wide_rows, wide_rows, wide_last, wide_last)
    return jax.shard_map(
        body,
        mesh=mesh,
        in_specs=(wide_ends, *dense, experts, experts, wide_ends),
        out_specs=(wide_ends, *dense, experts, experts),
        check_vma=False,
    )
```

time: 1510 us -> 453 us (0.30)
  blocking collectives: 531 us -> 0 us
  waiting for transfers between devices: 346 us -> 12 us
  Pallas kernels: 0 us -> 207 us
  local copies, waits for them, and re-layouts: 172 us -> 71.9 us
  matrix products: 224 us -> 130 us
  starting transfers between devices: 99.9 us -> 6.41 us
  other arithmetic: 100 us -> 15.4 us
    unnamed x1 -> x0, blocking collectives: 280 us -> none
    unnamed x4 -> x0, waiting for transfers between devices: 274 us -> none
    all_gather x3 -> x0, blocking collectives: 251 us -> none  [the longest x1 88.6 us: fetch_dense(): lax.all_gather(route_weight, 'wide', axis=1, tiled=True)]
    pallas_call x0 -> x10, Pallas kernels: none -> 207 us  [the longest x4 76.2 us: collect(): pl.pallas_call(collect_kernel, out_shape=jax.ShapeDtypeStruct((32, SLOTS,...]
    dot_general x78 -> x42, matrix products: 224 us -> 125 us  [the longest x2 22.4 us: forward_layer(): part = jnp.dot(activated, weight_out, preferred_element_type=jnp.float32)]
    all_to_all x12 -> x0, starting transfers between devices: 87.2 us -> none  [the longest x3 25.2 us: backward_layer(): lax.all_to_all(outgoing, 'wide', split_axis=0, concat_axis=0, tiled=True)]
    reduce_sum x28 -> x8, other arithmetic: 39.5 us -> 1.26 us  [the longest x1 0.94 us: backward_layer(): gate_grad = jnp.sum(combined * grad_out[:, None], axis=3).swapaxes(1, 2)]
    all_gather x2 -> x0, waiting for transfers between devices: 36.3 us -> none  [the longest x1 36.3 us: fetch_dense(): lax.all_gather(qkv_weight, 'wide', axis=1, tiled=True)]
  transfers between devices with their start and end apart: 19 -> 2, of which waited for: 11 -> 2; matrix products, arithmetic and copies ran while one was open for 14% -> 0% of each run, Pallas kernels for 0% -> 0%
where the time goes in v1:
time: 453 us; the launch traced here: 445 us
  Pallas kernels  207 us (46%)
  matrix products  130 us (29%)
  local copies, waits for them, and re-layouts  71.9 us (16%)
  other arithmetic  15.4 us (3%)
  waiting for transfers between devices  12 us (3%)
  starting transfers between devices  6.41 us (1%)
    pallas_call x4, Pallas kernels, collect(): pl.pallas_call(collect_kernel, out_shape=jax.ShapeDtypeStruct((32, SLOTS,...  76.2 us
    pallas_call x4, Pallas kernels, dispatch(): pl.pallas_call(dispatch_kernel, out_shape=jax.ShapeDtypeStruct((2, 32, SL...  72.5 us
    pallas_call x1, Pallas kernels, gather_blocks(): pl.pallas_call(gather_kernel, out_shape=jax.ShapeDtypeStruct((64, BLOCK,...  30 us
    pallas_call x1, Pallas kernels, scatter_blocks(): pl.pallas_call(scatter_kernel, out_shape=jax.ShapeDtypeStruct((BLOCK, 128...  28.3 us
    dot_general x2, matrix products, forward_layer(): part = jnp.dot(activated, weight_out, preferred_element_type=jnp.float32)  22.4 us
    dot_general x1, matrix products, forward_layer(): raised = jnp.dot(arrived, weight_in, preferred_element_type=jnp.float32)  18.1 us
    dot_general x2, matrix products, backward_layer(): jnp.einsum('nf,df->nd', raised_grad, weight_in, preferred_element_type=jn...  15 us
    unnamed x144, local copies, waits for them, and re-layouts  14.7 us
  transfers between devices with their start and end apart: 2, of which 2 were waited for; matrix products, arithmetic and copies ran while one was open for 0% of the time, Pallas kernels for 0%

profile of v1, /device:TPU:0, one launch (start us, length us, event | category | flops | bytes accessed | tf_op | source)
XLA Modules:
  0.0 445.3 jit_solution(7782347059924240177)
XLA Ops:
  4.1 30.0 %gather_blocks.1 = bf16[64,304,128]{2,1,0:T(8,128)(2,1)} custom-call(bf16[304,128]{1,0:T(8,128)(2,1)} %pad_maximum_fusion.7.block_ref), custom_call_target="tpu_custom_call" | custom-call | tf_op jit(solution)/shard_map/gather_blocks/pallas_call | solution.py:150
  34.1 2.8 fusion.216
  37.9 1.8 copy.314
  39.8 3.0 copy.315
  42.8 3.6 copy.508
  47.9 2.7 convolution_convert_fusion.1
  50.6 2.0 reshape.324
  52.7 2.7 fusion.218
  55.3 2.2 fusion.221
  57.5 2.4 convolution_multiply_fusion.6
  61.3 1.8 convolution_convert_fusion.5
  63.2 1.7 fusion.222
  69.1 1.5 fusion.71
  71.6 20.4 %dispatch.4 = bf16[2,32,16,768]{3,2,1,0:T(8,128)(2,1)} custom-call(bf16[32,16,768]{2,1,0:T(8,128)(2,1)} %bitcast.449), custom_call_target="tpu_custom_call" | custom-call | tf_op jit(solution)/shard_map/dispatch/pallas_call | solution.py:361
  92.0 19.8 %fusion.49 = bf16[1024,768]{1,0:T(8,128)(2,1)} fusion(bf16[1,1,1536,768]{3,2,1,0:T(8,128)(2,1)} %param.16, bf16[1024,768]{1,0:T(8,128)(2,1)} %bitcast.456, bf16[1,1,768,1536]{3,2,1,0:T(8,128)(2,1)S(1)} %copy-done), kind=kOutput, calls=%fused_computation.73 | convolution fusion | flops 4934860800 | bytes 7864320 | tf_op jit(solution)/shard_map/dot_general | solution.py:593
  111.8 1.4 copy-done.1
  113.2 19.0 %collect.4 = bf16[32,16,768]{2,1,0:T(8,128)(2,1)S(1)} custom-call(bf16[2,32,16,768]{3,2,1,0:T(8,128)(2,1)S(1)} %bitcast.426), custom_call_target="tpu_custom_call" | custom-call | tf_op jit(solution)/shard_map/collect/pallas_call | solution.py:435
  132.6 5.1 %collective-permute-start = (bf16[2,64,768]{2,1,0:T(8,128)(2,1)S(1)}, bf16[2,64,768]{2,1,0:T(8,128)(2,1)S(1)}, u32[]{:S(2)}, u32[]{:S(2)}) collective-permute-start(bf16[2,64,768]{2,1,0:T(8,128)(2,1)S(1)} %add_convert_fusion.6), channel_id=1, source_target_pairs={{0,64},{1,65},{2,66},{3,67},{4,68},{5,69},{6,70},{7,71},{8,72},{9,... | collective-permute-start | bytes 589832 | tf_op jit(solution)/shard_map/ppermute | solution.py:460
  138.5 3.0 collective-permute-done
  141.9 3.5 convolution_convert_fusion
  145.4 3.2 reshape.333
  148.6 2.6 fusion.217
  151.2 1.4 copy.431
  152.6 2.7 fusion.223
  155.2 1.4 convolution_convert_fusion.4
  157.4 1.7 fusion.224
  162.5 17.0 %dispatch.5 = bf16[2,32,16,768]{3,2,1,0:T(8,128)(2,1)} custom-call(bf16[32,16,768]{2,1,0:T(8,128)(2,1)} %bitcast.450), custom_call_target="tpu_custom_call" | custom-call | tf_op jit(solution)/shard_map/dispatch/pallas_call | solution.py:361
  179.5 18.1 %multiply_convert_fusion = (bf16[1024,1536]{1,0:T(8,128)(2,1)S(1)}, f32[1024,1536]{1,0:T(8,128)}, f32[1024,1536]{1,0:T(8,128)}) fusion(bf16[1024,768]{1,0:T(8,128)(2,1)} %bitcast.447, bf16[1,1,768,1536]{3,2,1,0:T(8,128)(2,1)S(1)} %copy-done), kind=kOutput, calls=%fused_computation.14 | convolution fusion | flops 2518155264 | bytes 19660800 | tf_op jit(solution)/shard_map/dot_general | solution.py:591
  197.7 2.6 fusion.64
  200.3 19.1 %collect.5 = bf16[32,16,768]{2,1,0:T(8,128)(2,1)S(1)} custom-call(bf16[2,32,16,768]{3,2,1,0:T(8,128)(2,1)S(1)} %bitcast.428), custom_call_target="tpu_custom_call" | custom-call | tf_op jit(solution)/shard_map/collect/pallas_call | solution.py:435
  222.2 17.9 %dispatch.6 = bf16[2,32,16,768]{3,2,1,0:T(8,128)(2,1)} custom-call(bf16[32,16,768]{2,1,0:T(8,128)(2,1)} %bitcast.451), custom_call_target="tpu_custom_call" | custom-call | tf_op jit(solution)/shard_map/dispatch/pallas_call | solution.py:361
  240.0 12.3 %fusion.56 = bf16[1024,768]{1,0:T(8,128)(2,1)} fusion(bf16[1,1,768,1536]{3,2,1,0:T(8,128)(2,1)S(1)} %copy-done, f32[1024,1536]{1,0:T(8,128)} %get-tuple-element.67, f32[1024,1536]{1,0:T(8,128)} %get-tuple-element.92, bf16[1024,768]{1,0:T(8,128)(2,1)} %bitcast.455, bf16[1,1,1536,768]{3,2,1,0:T(8,128)(2,1)} %param.16), kind=kOutput, calls=%fused_computation.74 | convolution fusion | flops 4854644736 | bytes 20447232 | tf_op jit(solution)/shard_map/nf,df->nd/dot_general | solution.py:630
  252.4 1.4 copy-done.2
  253.8 19.1 %collect.6 = bf16[32,16,768]{2,1,0:T(8,128)(2,1)S(1)} custom-call(bf16[2,32,16,768]{3,2,1,0:T(8,128)(2,1)S(1)} %bitcast.427), custom_call_target="tpu_custom_call" | custom-call | tf_op jit(solution)/shard_map/collect/pallas_call | solution.py:435
  274.5 1.8 convolution_convert_fusion.7
  277.3 1.7 fusion.80
  279.0 1.7 multiply_reduce_fusion.3
  281.8 2.0 copy.352
  283.8 3.2 convert_element_type.191
  287.0 3.7 fusion.212
  291.8 1.3 collective-permute-start.1
  293.1 9.0 %collective-permute-done.1 = bf16[2,64,768]{2,1,0:T(8,128)(2,1)S(1)} collective-permute-done((bf16[2,64,768]{2,1,0:T(8,128)(2,1)S(1)}, bf16[2,64,768]{2,1,0:T(8,128)(2,1)S(1)}, u32[]{:S(2)}, u32[]{:S(2)}) %collective-permute-start.1) | collective-permute-done | bytes 196640 | tf_op jit(solution)/shard_map/ppermute | solution.py:460
  305.1 17.3 %dispatch.7 = bf16[2,32,16,768]{3,2,1,0:T(8,128)(2,1)} custom-call(bf16[32,16,768]{2,1,0:T(8,128)(2,1)} %bitcast.452), custom_call_target="tpu_custom_call" | custom-call | tf_op jit(solution)/shard_map/dispatch/pallas_call | solution.py:361
  322.4 9.8 %add_convert_fusion = bf16[1024,1536]{1,0:T(8,128)(2,1)S(1)} fusion(f32[1024,1536]{1,0:T(8,128)} %get-tuple-element.67, f32[1024,1536]{1,0:T(8,128)} %get-tuple-element.92, bf16[1024,768]{1,0:T(8,128)(2,1)} %bitcast.453, bf16[1,1,1536,768]{3,2,1,0:T(8,128)(2,1)} %param.16), kind=kOutput, calls=%fused_computation.12 | convolution fusion | flops 2437939200 | bytes 19660800 | tf_op jit(solution)/shard_map/nd,fd->nf/dot_general | solution.py:626
  332.3 2.6 fusion.61
  334.9 19.1 %collect.7 = bf16[32,16,768]{2,1,0:T(8,128)(2,1)S(1)} custom-call(bf16[2,32,16,768]{3,2,1,0:T(8,128)(2,1)S(1)} %bitcast.429), custom_call_target="tpu_custom_call" | custom-call | tf_op jit(solution)/shard_map/collect/pallas_call | solution.py:435
  355.7 1.8 convolution_convert_fusion.6
  358.4 1.7 fusion.81
  360.2 1.7 multiply_reduce_fusion.1
  362.7 1.5 bitcast_convert_fusion.1
  364.6 2.0 copy.367
  366.5 3.0 convert_element_type.201
  369.6 5.0 %fusion.125 = (bf16[768]{0:T(1024)(128)(2,1)}, f32[2,64]{1,0:T(2,128)}, f32[2,64]{1,0:T(2,128)}, bf16[768]{0:T(1024)(128)(2,1)}, f32[2,64,768]{2,1,0:T(8,128)}) fusion(bf16[2,64,768]{2,1,0:T(8,128)(2,1)S(1)} %get-tuple-element.69, f32[2,64]{1,0:T(2,128)S(1)} %copy-done.50, f32[2,64]{1,0:T(2,128)S(1)} %copy-done.46, f32[768]{0:T(1024)S(1)} %copy-done.39, ...), kind=kOutput, calls=%fused_computation.179 | convolution fusion | flops 453966080 | bytes 4726784 | tf_op jit(solution)/shard_map/bte,de->btd/dot_general | solution.py:672
  374.6 1.2 bitcast_convert_fusion
  377.4 1.4 copy.438
  378.8 1.8 copy.370
  380.7 5.2 %copy.378 = bf16[2,4,4,2,288,128]{5,4,1,2,3,0:T(8,128)(2,1)} copy(bf16[2,4,4,2,288,128]{5,3,2,1,0,4:T(2,128)(2,1)S(1)} %bitcast.437) | data formatting | bytes 9437184 | tf_op jit(solution)/shard_map/concatenate | solution.py:521
  389.4 1.9 concatenate.51
  392.3 2.8 maximum_bitcast_fusion
  396.0 28.3 %scatter_blocks.1 = f32[304,128]{1,0:T(8,128)S(1)} custom-call(bf16[2,2,4,4,304,128]{5,4,3,2,1,0:T(8,128)(2,1)S(1)} %pad_maximum_fusion.1.parts_ref), custom_call_target="tpu_custom_call" | custom-call | tf_op jit(solution)/shard_map/scatter_blocks/pallas_call | solution.py:280
  424.9 1.6 reshape.357
  427.8 7.4 %convolution_bitcast_fusion.1 = f32[1,1,768,1536]{3,2,1,0:T(8,128)} fusion(bf16[1024,768]{1,0:T(8,128)(2,1)} %bitcast.448, bf16[1024,1536]{1,0:T(8,128)(2,1)} %copy-done.14), kind=kOutput, calls=%fused_computation.50 | convolution fusion | flops 2415919104 | bytes 9437184 | tf_op jit(solution)/shard_map/nd,nf->df/dot_general | solution.py:629
  435.3 4.4 convolution_bitcast_fusion
  443.1 2.0 fusion.153
  (267 shorter events, 44.2 us)
Async XLA Ops:
  0.6 91.4 %copy-start = (bf16[1,1,768,1536]{3,2,1,0:T(8,128)(2,1)S(1)}, bf16[1,1,768,1536]{3,2,1,0:T(8,128)(2,1)}, u32[]{:S(2)}) copy-start(bf16[1,1,768,1536]{3,2,1,0:T(8,128)(2,1)} %param.15) | copy-start | bytes 7077892
  37.5 2.2 copy-start.3
  42.8 4.7 %copy-start.4 = (bf16[1,2,64,768]{3,2,1,0:T(8,128)(2,1)S(1)}, bf16[1,2,64,768]{3,2,1,0:T(8,128)(2,1)}, u32[]{:S(2)}) copy-start(bf16[1,2,64,768]{3,2,1,0:T(8,128)(2,1)} %param.9) | copy-start | bytes 589828
  47.4 94.5 %copy-start.52 = (f32[768]{0:T(1024)}, f32[768]{0:T(1024)S(1)}, u32[]{:S(2)}) copy-start(f32[768]{0:T(1024)S(1)} %add.102) | copy-start | bytes 9220
  47.6 94.3 %copy-start.37 = (f32[768]{0:T(1024)}, f32[768]{0:T(1024)S(1)}, u32[]{:S(2)}) copy-start(f32[768]{0:T(1024)S(1)} %mul.387) | copy-start | bytes 9220
  61.3 6.1 %copy-start.58 = (s32[1,2,64,2]{2,3,1,0:T(2,128)S(1)}, s32[1,2,64,2]{2,3,1,0:T(2,128)}, u32[]{:S(2)}) copy-start(s32[1,2,64,2]{2,3,1,0:T(2,128)} %param.17) | copy-start | bytes 3076
  69.1 63.1 %copy-start.41 = (s32[2,2,64]{2,1,0:T(2,128)}, s32[2,2,64]{2,1,0:T(2,128)S(1)}, u32[]{:S(2)}) copy-start(s32[2,2,64]{2,1,0:T(2,128)S(1)} %copy.325) | copy-start | bytes 3076
  111.8 1.4 copy-start.1
  132.6 9.0 %collective-permute-start = (bf16[2,64,768]{2,1,0:T(8,128)(2,1)S(1)}, bf16[2,64,768]{2,1,0:T(8,128)(2,1)S(1)}, u32[]{:S(2)}, u32[]{:S(2)}) collective-permute-start(bf16[2,64,768]{2,1,0:T(8,128)(2,1)S(1)} %add_convert_fusion.6), channel_id=1, source_target_pairs={{0,64},{1,65},{2,66},{3,67},{4,68},{5,69},{6,70},{7,71},{8,72},{9,... | collective-permute-start | bytes 589832 | tf_op jit(solution)/shard_map/ppermute | solution.py:460
  141.7 9.5 %copy-start.44 = (f32[2,64]{1,0:T(2,128)}, f32[2,64]{1,0:T(2,128)S(1)}, u32[]{:S(2)}) copy-start(f32[2,64]{1,0:T(2,128)S(1)} %broadcast_multiply_fusion.9) | copy-start | bytes 1540
  141.9 9.3 %copy-start.48 = (f32[2,64]{1,0:T(2,128)}, f32[2,64]{1,0:T(2,128)S(1)}, u32[]{:S(2)}) copy-start(f32[2,64]{1,0:T(2,128)S(1)} %add_rsqrt_fusion.1) | copy-start | bytes 1540
  152.6 4.1 copy-start.23
  155.2 4.1 copy-start.27
  156.7 0.8 copy-start.21
  159.4 38.3 %copy-start.30 = (f32[2,64]{1,0:T(2,128)}, f32[2,64]{1,0:T(2,128)S(1)}, u32[]{:S(2)}) copy-start(f32[2,64]{1,0:T(2,128)S(1)} %add_rsqrt_fusion) | copy-start | bytes 1540
  179.5 18.2 %copy-start.63 = (bf16[1,1,1536,768]{3,2,1,0:T(8,128)(2,1)S(1)}, bf16[1,1,1536,768]{3,2,1,0:T(8,128)(2,1)}, u32[]{:S(2)}) copy-start(bf16[1,1,1536,768]{3,2,1,0:T(8,128)(2,1)} %param.16) | copy-start | bytes 7077892
  197.6 2.7 copy-start.64
  197.6 21.7 %copy-start.26 = (f32[2,64,32]{1,2,0:T(8,128)S(1)}, f32[2,64,32]{1,2,0:T(8,128)}, u32[]{:S(2)}) copy-start(f32[2,64,32]{1,2,0:T(8,128)} %fusion.142) | copy-start | bytes 49156
  197.7 21.7 %copy-start.35 = (s32[2,64,2]{1,2,0:T(2,128)S(1)}, s32[2,64,2]{1,2,0:T(2,128)}, u32[]{:S(2)}) copy-start(s32[2,64,2]{1,2,0:T(2,128)} %copy-done.34) | copy-start | bytes 3076
  197.7 21.8 %copy-start.8 = (f32[2,64,768]{2,1,0:T(8,128)S(1)}, f32[2,64,768]{2,1,0:T(8,128)}, u32[]{:S(2)}) copy-start(f32[2,64,768]{2,1,0:T(8,128)} %bitcast_convert_fusion.6) | copy-start | bytes 1179652
  197.7 21.8 %copy-start.42 = (s32[2,2,64]{2,1,0:T(2,128)S(1)}, s32[2,2,64]{2,1,0:T(2,128)}, u32[]{:S(2)}) copy-start(s32[2,2,64]{2,1,0:T(2,128)} %copy-done.41) | copy-start | bytes 3076
  240.0 33.2 %copy-start.31 = (f32[2,64]{1,0:T(2,128)S(1)}, f32[2,64]{1,0:T(2,128)}, u32[]{:S(2)}) copy-start(f32[2,64]{1,0:T(2,128)} %copy-done.30) | copy-start | bytes 1540
  252.4 1.4 copy-start.2
  277.3 3.4 copy-start.15
  277.3 3.5 copy-start.28
  277.3 3.7 copy-start.11
  277.3 3.9 copy-start.9
  280.7 6.3 %copy-start.38 = (f32[768]{0:T(1024)S(1)}, f32[768]{0:T(1024)}, u32[]{:S(2)}) copy-start(f32[768]{0:T(1024)} %copy-done.37) | copy-start | bytes 9220
  280.7 6.3 %copy-start.45 = (f32[2,64]{1,0:T(2,128)S(1)}, f32[2,64]{1,0:T(2,128)}, u32[]{:S(2)}) copy-start(f32[2,64]{1,0:T(2,128)} %copy-done.44) | copy-start | bytes 1540
  280.7 6.3 %copy-start.49 = (f32[2,64]{1,0:T(2,128)S(1)}, f32[2,64]{1,0:T(2,128)}, u32[]{:S(2)}) copy-start(f32[2,64]{1,0:T(2,128)} %copy-done.48) | copy-start | bytes 1540
  287.0 3.7 copy-start.20
  287.0 16.2 %copy-start.13 = (f32[2,2,64,768]{3,2,1,0:T(8,128)S(1)}, f32[2,2,64,768]{3,2,1,0:T(8,128)}, u32[]{:S(2)}) copy-start(f32[2,2,64,768]{3,2,1,0:T(8,128)} %get-tuple-element.94) | copy-start | bytes 2359300
  291.8 10.3 %collective-permute-start.1 = (bf16[2,64,768]{2,1,0:T(8,128)(2,1)S(1)}, bf16[2,64,768]{2,1,0:T(8,128)(2,1)S(1)}, u32[]{:S(2)}, u32[]{:S(2)}) collective-permute-start(bf16[2,64,768]{2,1,0:T(8,128)(2,1)S(1)} %fusion.118), channel_id=1, source_target_pairs={{64,0},{65,1},{66,2},{67,3},{68,4},{69,5},{70,6},{71,7},{72,8},{73... | collective-permute-start | bytes 589832 | tf_op jit(solution)/shard_map/ppermute | solution.py:460
  302.1 1.2 copy-start.5
  332.2 2.7 copy-start.14
  332.2 21.8 %copy-start.43 = (s32[2,2,64]{2,1,0:T(2,128)S(1)}, s32[2,2,64]{2,1,0:T(2,128)}, u32[]{:S(2)}) copy-start(s32[2,2,64]{2,1,0:T(2,128)} %copy-done.41) | copy-start | bytes 3076
  332.3 22.1 %copy-start.36 = (s32[2,64,2]{1,2,0:T(2,128)S(1)}, s32[2,64,2]{1,2,0:T(2,128)}, u32[]{:S(2)}) copy-start(s32[2,64,2]{1,2,0:T(2,128)} %copy-done.34) | copy-start | bytes 3076
  332.3 22.1 %copy-start.32 = (f32[2,64]{1,0:T(2,128)S(1)}, f32[2,64]{1,0:T(2,128)}, u32[]{:S(2)}) copy-start(f32[2,64]{1,0:T(2,128)} %copy-done.30) | copy-start | bytes 1540
  332.3 23.2 %copy-start.6 = (f32[2,64,768]{2,1,0:T(8,128)S(1)}, f32[2,64,768]{2,1,0:T(8,128)}, u32[]{:S(2)}) copy-start(f32[2,64,768]{2,1,0:T(8,128)} %copy-done.5) | copy-start | bytes 1179652
  354.4 1.1 copy-start.24
  358.4 3.4 copy-start.16
  358.4 3.5 copy-start.29
  358.4 3.7 copy-start.12
  358.4 4.0 copy-start.10
  358.4 4.3 copy-start.22
  362.1 7.4 %copy-start.39 = (f32[768]{0:T(1024)S(1)}, f32[768]{0:T(1024)}, u32[]{:S(2)}) copy-start(f32[768]{0:T(1024)} %copy-done.37) | copy-start | bytes 9220
  362.1 7.4 %copy-start.46 = (f32[2,64]{1,0:T(2,128)S(1)}, f32[2,64]{1,0:T(2,128)}, u32[]{:S(2)}) copy-start(f32[2,64]{1,0:T(2,128)} %copy-done.44) | copy-start | bytes 1540
  362.1 7.4 %copy-start.50 = (f32[2,64]{1,0:T(2,128)S(1)}, f32[2,64]{1,0:T(2,128)}, u32[]{:S(2)}) copy-start(f32[2,64]{1,0:T(2,128)} %copy-done.48) | copy-start | bytes 1540
  364.3 10.3 %copy-start.53 = (f32[768]{0:T(1024)S(1)}, f32[768]{0:T(1024)}, u32[]{:S(2)}) copy-start(f32[768]{0:T(1024)} %copy-done.52) | copy-start | bytes 9220
  366.5 9.3 %copy-start.25 = (f32[2,64,32]{1,2,0:T(8,128)S(1)}, f32[2,64,32]{1,2,0:T(8,128)}, u32[]{:S(2)}) copy-start(f32[2,64,32]{1,2,0:T(8,128)} %copy-done.24) | copy-start | bytes 49156
  366.5 9.3 %copy-start.33 = (f32[2,64]{1,0:T(2,128)S(1)}, f32[2,64]{1,0:T(2,128)}, u32[]{:S(2)}) copy-start(f32[2,64]{1,0:T(2,128)} %copy-done.30) | copy-start | bytes 1540
  369.6 5.0 %copy-start.17 = (bf16[2,64,2304]{2,1,0:T(8,128)(2,1)S(1)}, bf16[2,64,2304]{2,1,0:T(8,128)(2,1)}, u32[]{:S(2)}) copy-start(bf16[2,64,2304]{2,1,0:T(8,128)(2,1)} %convert_element_type.201) | copy-start | bytes 1769476
  369.6 7.2 %copy-start.7 = (bf16[768,768]{1,0:T(8,128)(2,1)S(1)}, bf16[768,768]{1,0:T(8,128)(2,1)}, u32[]{:S(2)}) copy-start(bf16[768,768]{1,0:T(8,128)(2,1)} %bitcast_convert_fusion.1) | copy-start | bytes 3538948
  380.6 7.0 %copy-start.55 = (bf16[768]{0:T(1024)(128)(2,1)S(1)}, bf16[768]{0:T(1024)(128)(2,1)}, u32[]{:S(2)}) copy-start(bf16[768]{0:T(1024)(128)(2,1)} %get-tuple-element.57) | copy-start | bytes 4612
  380.6 7.2 %copy-start.60 = (bf16[768]{0:T(1024)(128)(2,1)S(1)}, bf16[768]{0:T(1024)(128)(2,1)}, u32[]{:S(2)}) copy-start(bf16[768]{0:T(1024)(128)(2,1)} %get-tuple-element.56) | copy-start | bytes 4612
  380.6 7.4 %copy-start.54 = (bf16[768]{0:T(1024)(128)(2,1)S(1)}, bf16[768]{0:T(1024)(128)(2,1)}, u32[]{:S(2)}) copy-start(bf16[768]{0:T(1024)(128)(2,1)} %get-tuple-element.48) | copy-start | bytes 4612
  380.6 7.7 %copy-start.59 = (bf16[768]{0:T(1024)(128)(2,1)S(1)}, bf16[768]{0:T(1024)(128)(2,1)}, u32[]{:S(2)}) copy-start(bf16[768]{0:T(1024)(128)(2,1)} %get-tuple-element.52) | copy-start | bytes 4612
  426.5 8.7 %copy-start.18 = (bf16[2,32,16,768]{3,2,1,0:T(8,128)(2,1)S(1)}, bf16[2,32,16,768]{3,2,1,0:T(8,128)(2,1)}, u32[]{:S(2)}) copy-start(bf16[2,32,16,768]{3,2,1,0:T(8,128)(2,1)} %dispatch.7) | copy-start | bytes 4718596
  426.5 8.7 %copy-start.65 = (bf16[1024,1536]{1,0:T(8,128)(2,1)S(1)}, bf16[1024,1536]{1,0:T(8,128)(2,1)}, u32[]{:S(2)}) copy-start(bf16[1024,1536]{1,0:T(8,128)(2,1)} %copy-done.64) | copy-start | bytes 9437188
  435.2 4.4 copy-start.62
  435.2 4.4 copy-start.61
  435.2 7.8 %copy-start.40 = (f32[768]{0:T(1024)S(1)}, f32[768]{0:T(1024)}, u32[]{:S(2)}) copy-start(f32[768]{0:T(1024)} %copy-done.37) | copy-start | bytes 9220
  435.2 7.8 %copy-start.47 = (f32[2,64]{1,0:T(2,128)S(1)}, f32[2,64]{1,0:T(2,128)}, u32[]{:S(2)}) copy-start(f32[2,64]{1,0:T(2,128)} %copy-done.44) | copy-start | bytes 1540
  435.3 7.8 %copy-start.51 = (f32[2,64]{1,0:T(2,128)S(1)}, f32[2,64]{1,0:T(2,128)}, u32[]{:S(2)}) copy-start(f32[2,64]{1,0:T(2,128)} %copy-done.48) | copy-start | bytes 1540
  (4 other events, 2.8 us)
